TPU v7x, 512 devices: a whole 4x8x8 slice. The times are simulated.
512 devices in a mesh: rep: 16 (over y, x_hi), fsdp: 32 (over z, x_lo, core).
Axes of the slice: x: 4 (x_hi: 2, x_lo: 2; x = x_hi * 2 + x_lo), y: 8, z: 8, core: 2. Of those that a mesh axis runs over, the one named last changes fastest.
Arguments:
- gradient: bfloat16 [16, 5120, 4096], P('rep', 'fsdp'), may hold values from -4 to 4
- momentum: bfloat16 [16, 5120, 4096], P('rep', 'fsdp'), may hold values from -2 to 2
- pseudo_gradient: bfloat16 [16, 5120, 1024], P('rep', 'fsdp'), may hold values from -8 to 8
- outer_momentum: bfloat16 [5120, 1024], P('fsdp'), may hold values from -6 to 6
Outputs:
- update: bfloat16 [16, 5120, 4096], P('rep', 'fsdp')
- renewed: bfloat16 [5120, 1024], P('fsdp')
All inputs are finite; a program needn't handle non-finite values.
Results may differ from a plain program's by a relative error of at most 0.014.
Values may be sent and summed in bfloat16 or wider, within the bound.
A program may use at most 64 MiB of HBM per device.

v0:
```python
import math

import jax
import jax.numpy as jnp
from jax import lax
from jax.sharding import PartitionSpec as P

HD = 128
ITERS = 5


quint_a = 3.4445
quint_b = -4.775
quint_c = 2.0315
inner_beta = 0.95
outer_beta = 0.9
norm_eps = 1e-07
highest = lax.Precision.HIGHEST


def nesterov_input(gradient, momentum):
    grad_wide = gradient.astype(jnp.float32)
    velocity = inner_beta * momentum.astype(jnp.float32) + grad_wide
    return (grad_wide + inner_beta * velocity).astype(jnp.bfloat16)


def orthogonal_items(nesterov):
    matrix = nesterov.astype(jnp.float32)
    square = jnp.sum(matrix * matrix, axis=(0, 3), keepdims=True)
    matrix = matrix / (jnp.sqrt(square) + norm_eps)
    for sweep_index in range(ITERS):
        gram_matrix = jnp.einsum(
            "dapi,dapj->apij", matrix, matrix, precision=highest, preferred_element_type=jnp.float32
        )
        polynomial = quint_b * gram_matrix + quint_c * jnp.einsum(
            "apij,apjk->apik",
            gram_matrix,
            gram_matrix,
            precision=highest,
            preferred_element_type=jnp.float32,
        )
        matrix = quint_a * matrix + jnp.einsum(
            "dapi,apij->dapj",
            matrix,
            polynomial,
            precision=highest,
            preferred_element_type=jnp.float32,
        )
    scaled = (math.sqrt(matrix.shape[0]) * matrix).astype(jnp.bfloat16)
    return lax.all_to_all(scaled, "fsdp", split_axis=0, concat_axis=1, tiled=True)


def owner_work(pieces):
    return orthogonal_items(nesterov_input(pieces[0], pieces[1]))


def shards(gradient, momentum, pseudo_gradient, outer_momentum):
    owners = lax.axis_size("fsdp")
    row_count = gradient.shape[1]
    features = gradient.shape[2]
    per_owner = features // (owners * HD)
    layout = (row_count, owners, per_owner, HD)
    update = owner_work(
        (
            lax.all_to_all(
                gradient.reshape(layout), "fsdp", split_axis=1, concat_axis=0, tiled=True
            ),
            lax.all_to_all(
                momentum.reshape(layout), "fsdp", split_axis=1, concat_axis=0, tiled=True
            ),
        )
    )
    update = update.reshape(1, row_count, features)
    replicas = lax.axis_size("rep")
    pseudo_terms = pseudo_gradient[0].astype(jnp.float32)
    summed = lax.psum(pseudo_terms.astype(jnp.bfloat16), "rep").astype(jnp.float32)
    renewed = (outer_beta * outer_momentum.astype(jnp.float32) + summed / replicas).astype(
        jnp.bfloat16
    )
    return (update, renewed)


def solution(mesh):
    return jax.shard_map(
        shards,
        mesh=mesh,
        in_specs=(
            P("rep", "fsdp", None),
            P("rep", "fsdp", None),
            P("rep", "fsdp", None),
            P("fsdp", None),
        ),
        out_specs=(P("rep", "fsdp", None), P("fsdp", None)),
        check_vma=False,
    )
```

profile of v0, /device:TPU:8, one launch (start us, length us, event | category | flops | bytes accessed | tf_op | source)
XLA Modules:
  0.0 334.2 jit_solution(7301421470757583786)
XLA Ops:
  7.2 1.6 copy.46
  8.8 0.0 copy-start.2
  8.8 1.6 copy.32
  10.3 11.6 %all-to-all-start = ((bf16[160,32,1,128]{3,0,2,1:T(8,128)(2,1)}), bf16[160,32,1,128]{3,0,2,1:T(8,128)(2,1)S(1)}, u32[]{:S(2)}, u32[]{:S(2)}) async-start(bf16[160,32,1,128]{3,0,2,1:T(8,128)(2,1)} %copy.32), calls=%async_computation | async-start | bytes 2621440 | tf_op jit(solution)/shard_map/all_to_all | solution.py:65
  22.0 0.0 copy-done.2
  22.0 0.3 copy.47
  22.3 1.6 copy.34
  23.9 32.2 %all-to-all-done = bf16[160,32,1,128]{3,0,2,1:T(8,128)(2,1)S(1)} async-done(((bf16[160,32,1,128]{3,0,2,1:T(8,128)(2,1)}), bf16[160,32,1,128]{3,0,2,1:T(8,128)(2,1)S(1)}, u32[]{:S(2)}, u32[]{:S(2)}) %all-to-all-start) | async-done | bytes 1310752 | tf_op jit(solution)/shard_map/all_to_all | solution.py:65
  56.0 38.7 %all_to_all.33 = bf16[160,32,1,128]{3,0,2,1:T(8,128)(2,1)S(1)} all-to-all(bf16[160,32,1,128]{3,0,2,1:T(8,128)(2,1)} %copy.34), channel_id=1, replica_groups=mesh['rep'=16,'fsdp'=32] {'fsdp'}, dimensions={1} | all-to-all | bytes 2621440 | tf_op jit(solution)/shard_map/all_to_all | solution.py:68
  94.8 1.3 fusion.7
  96.7 0.6 convert_divide_fusion
  97.3 0.0 copy-start
  97.3 4.4 %fusion.30 = f32[128,128]{1,0:T(8,128)S(1)} fusion(f32[32,160,1,1,128]{4,1,0,3,2:T(8,128)S(1)} %convert_divide_fusion), kind=kOutput, calls=%fused_computation.46 | convolution fusion | flops 1006632960 | bytes 2686976 | tf_op jit(solution)/shard_map/dapi,dapj->apij/dot_general | solution.py:32
  101.8 0.2 fusion.29
  102.0 1.8 convert_multiply_fusion.1
  103.8 0.0 copy-done
  103.8 3.2 copy.36
  107.0 1.9 bitcast_convert_fusion
  108.9 0.0 copy-start.1
  108.9 3.4 %copy.38 = f32[5120,1,1,128]{0,3,2,1:T(8,128)} copy(f32[5120,1,1,128]{3,0,2,1:T(8,128)} %bitcast.141) | data formatting | bytes 5242880 | tf_op jit(solution)/shard_map/convert_element_type | solution.py:22
  112.3 0.0 copy-done.1
  112.3 5.4 %fusion = f32[5120,1,1,128]{0,3,2,1:T(8,128)S(1)} fusion(f32[128,128]{1,0:T(8,128)S(1)} %fusion.29, f32[5120,128]{1,0:T(8,128)S(1)} %bitcast.139, f32[5120,1,1,128]{0,3,2,1:T(8,128)} %copy.38, f32[5120,1,1,128]{0,3,2,1:T(8,128)} %copy.36, f32[]{:T(128)S(6)} %add.92), kind=kOutput, calls=%fused_computation.5 | convolution fusion | flops 1011875840 | bytes 10551300 | tf_op jit(solution)/shard_map/dapi,apij->dapj/dot_general | solution.py:42
  117.7 2.2 fusion.18
  119.9 0.2 fusion.28
  120.1 2.7 fusion.1
  122.8 2.2 fusion.15
  125.0 0.2 fusion.27
  125.2 2.9 fusion.2
  128.2 2.2 fusion.12
  130.4 0.2 fusion.26
  130.6 2.7 fusion.3
  133.2 2.2 fusion.9
  135.5 0.2 fusion.25
  135.7 2.7 fusion.6
  138.4 0.5 broadcast.130
  138.9 1.6 reduce.2
  140.5 0.8 copy.48
  141.3 0.0 copy-start.3
  141.3 1.2 reshape.206
  142.5 4.7 %all-to-all-start.2 = ((bf16[32,2,10240]{2,1,0:T(2,128)(2,1)}), bf16[32,2,10240]{2,1,0:T(2,128)(2,1)}, u32[]{:S(2)}, u32[]{:S(2)}) async-start(bf16[32,2,10240]{2,1,0:T(2,128)(2,1)} %reshape.206), calls=%async_computation.2 | async-start | bytes 2621440 | tf_op jit(solution)/shard_map/all_to_all | solution.py:50
  147.2 0.0 all-reduce.2.cloned.1.call-start
  147.2 0.7 all-reduce.2.cloned.1.call-update
  147.9 167.8 %all-reduce.2.cloned.1.call-done = bf16[160,1024]{1,0:T(8,128)(2,1)} async-done(((bf16[160,1024]{1,0:T(8,128)(2,1)}), bf16[160,1024]{1,0:T(8,128)(2,1)}) %all-reduce.2.cloned.1.call-update) | async-done | bytes 327696 | tf_op jit(solution)/shard_map/psum | solution.py:76
  315.7 0.0 copy-done.3
  315.7 1.8 add_convert_fusion.1
  317.5 0.0 all-to-all-done.2
  317.5 7.7 %reshape.207 = bf16[5120,1,1,128]{3,2,1,0:T(2,128)(2,1)S(1)} reshape(bf16[32,2,10240]{2,1,0:T(2,128)(2,1)} %all-to-all-done.2) | data formatting | bytes 2621440
  325.2 0.2 copy.45
  325.4 0.5 copy.42
  325.9 1.4 reshape.201
Async XLA Ops:
  8.8 13.2 %copy-start.2 = (bf16[1,160,4096]{2,1,0:T(8,128)(2,1)S(1)}, bf16[1,160,4096]{2,1,0:T(8,128)(2,1)}, u32[]{:S(2)}) copy-start(bf16[1,160,4096]{2,1,0:T(8,128)(2,1)} %param.5) | copy-start | bytes 3932164
  10.3 45.7 %all-to-all-start = ((bf16[160,32,1,128]{3,0,2,1:T(8,128)(2,1)}), bf16[160,32,1,128]{3,0,2,1:T(8,128)(2,1)S(1)}, u32[]{:S(2)}, u32[]{:S(2)}) async-start(bf16[160,32,1,128]{3,0,2,1:T(8,128)(2,1)} %copy.32), calls=%async_computation | async-start | bytes 2621440 | tf_op jit(solution)/shard_map/all_to_all | solution.py:65
  97.3 6.5 %copy-start = (f32[32,160,1,1,128]{4,1,0,3,2:T(8,128)}, f32[32,160,1,1,128]{4,1,0,3,2:T(8,128)S(1)}, u32[]{:S(2)}) copy-start(f32[32,160,1,1,128]{4,1,0,3,2:T(8,128)S(1)} %convert_divide_fusion) | copy-start | bytes 7864324
  108.9 3.4 %copy-start.1 = (f32[32,160,1,1,128]{4,1,0,3,2:T(8,128)S(1)}, f32[32,160,1,1,128]{4,1,0,3,2:T(8,128)}, u32[]{:S(2)}) copy-start(f32[32,160,1,1,128]{4,1,0,3,2:T(8,128)} %copy-done) | copy-start | bytes 7864324
  141.3 174.4 %copy-start.3 = (bf16[160,1024]{1,0:T(8,128)(2,1)S(1)}, bf16[160,1024]{1,0:T(8,128)(2,1)}, u32[]{:S(2)}) copy-start(bf16[160,1024]{1,0:T(8,128)(2,1)} %param.7) | copy-start | bytes 983044
  142.5 175.0 %all-to-all-start.2 = ((bf16[32,2,10240]{2,1,0:T(2,128)(2,1)}), bf16[32,2,10240]{2,1,0:T(2,128)(2,1)}, u32[]{:S(2)}, u32[]{:S(2)}) async-start(bf16[32,2,10240]{2,1,0:T(2,128)(2,1)} %reshape.206), calls=%async_computation.2 | async-start | bytes 2621440 | tf_op jit(solution)/shard_map/all_to_all | solution.py:50
  147.2 168.5 %all-reduce.2.cloned.1.call-start = ((), (), s32[]{:S(2)}) async-start(), calls=%async_computation.3 | async-start | bytes 655360 | tf_op jit(solution)/shard_map/psum | solution.py:76
Sparse Core Ops, SparseCore 0:
  151.0 164.6 all-reduce.1
where the time goes:
time: 335 us; the launch traced here: 334 us
  waiting for transfers between devices  201 us (60%)
  blocking collectives  38.7 us (12%)
  matrix products  30.6 us (9%)
  local copies, waits for them, and re-layouts  24 us (7%)
  starting transfers between devices  16.4 us (5%)
  between operations  14.9 us (4%)
  other arithmetic  9 us (3%)
    psum x1, waiting for transfers between devices, shards(): lax.psum(pseudo_terms.astype(jnp.bfloat16), 'rep').astype(jnp.float32)  168 us
    all_to_all x1, blocking collectives, shards(): lax.all_to_all(momentum.reshape(layout), 'fsdp', split_axis=1, concat_axi...  38.7 us
    all_to_all x1, waiting for transfers between devices, shards(): lax.all_to_all(gradient.reshape(layout), 'fsdp', split_axis=1, concat_axi...  32.2 us
    dot_general x5, matrix products, orthogonal_items(): jnp.einsum('dapi,apij->dapj', matrix, polynomial, precision=highest, pref...  16.4 us
    dot_general x5, matrix products, orthogonal_items(): jnp.einsum('dapi,dapj->apij', matrix, matrix, precision=highest, preferre...  13.2 us
    unnamed x14, local copies, waits for them, and re-layouts  11.8 us
    all_to_all x1, starting transfers between devices, shards(): lax.all_to_all(gradient.reshape(layout), 'fsdp', split_axis=1, concat_axi...  11.6 us
  transfers between devices with their start and end apart: 3, of which 2 were waited for; matrix products, arithmetic and copies ran while one was open for 1% of the time, Pallas kernels for 0%

commit v1 on v0

v1 whole, which is shorter than its diff:
```python
import functools
import math

import jax
import jax.numpy as jnp
from jax import lax
from jax.experimental import pallas as pl
from jax.experimental.pallas import tpu as pltpu
from jax.sharding import PartitionSpec as P

HD = 128
HALF = HD // 2
PACK = HALF + 8
ITERS = 5

quint_a = 3.4445
quint_b = -4.775
quint_c = 2.0315
inner_beta = 0.95
outer_beta = 0.9
norm_eps = 1e-07
highest = lax.Precision.HIGHEST
f32 = jnp.float32
bf16 = jnp.bfloat16


def far_first(n):
    return sorted(range(n), key=lambda d: (-min(d, n - d), d))


def iota(axis, rows=HALF):
    return lax.broadcasted_iota(jnp.int32, (rows, HD), axis)


def masks():
    row, lane = iota(0), iota(1)
    upper = ((lane < HALF) & (lane >= row)) | ((lane >= HALF) & (lane - HALF < row))
    return upper, lane == row + HALF


def pack(full, upper, cross):
    top, low = full[:HALF], full[HALF:]
    diagonal = jnp.sum(jnp.where(cross, top, 0.0), axis=0, keepdims=True)
    return jnp.where(upper, top, low), jnp.broadcast_to(diagonal, (PACK - HALF, HD))


def spread(ref, upper, cross):
    body = ref[:HALF, :]
    top = jnp.where(upper, body, jnp.where(cross, ref[HALF : HALF + 1, :], 0.0))
    return jnp.concatenate([top, jnp.where(upper, 0.0, body)], axis=0)


def exact_dot(a, b):
    return jnp.dot(a, b, precision=highest, preferred_element_type=f32)


def kernel(
    nz, ny, grad, mom, pseudo, outer, update, renewed,
    gbuf, mbuf, oth, both, xs, xr, own, zr, mine, mz, mx, ms, out,
    yr, pself, pout, half_own, half_in, fresh,
    in_sem, core_sem, x_sem, z_sem, mz_sem, mx_sem, ms_sem, out_sem, y_sem, h_sem, r_sem, p_sem,
):
    rep, fsdp = lax.axis_index("rep"), lax.axis_index("fsdp")
    core, xl, z = fsdp % 2, (fsdp // 2) % 2, fsdp // 4
    xh, y = rep % 2, rep // 2
    rows, cols = oth.shape
    heads = cols // HD
    z_order, y_order = far_first(nz), far_first(ny)

    def at_z(d):
        return {"fsdp": (lax.rem(z + d, nz) * 2 + xl) * 2 + core}

    def at_y(d):
        return {"rep": lax.rem(y + d, ny) * 2 + xh}

    x_peer = {"fsdp": (z * 2 + (1 - xl)) * 2 + core}
    sibling = {"fsdp": (z * 2 + xl) * 2 + (1 - core)}
    h_peer = {"rep": y * 2 + (1 - xh)}
    z_peers = [at_z(d) for d in range(1, nz)]
    y_peers = [at_y(d) for d in range(1, ny)]
    everyone = [sibling, x_peer, h_peer] + z_peers + y_peers

    barrier = pltpu.get_barrier_semaphore()
    for peer in everyone:
        pl.semaphore_signal(barrier, inc=1, device_id=peer, device_id_type=pl.DeviceIdType.MESH)

    def remote(src, dst, sems, i, peer):
        return pltpu.make_async_remote_copy(
            src_ref=src, dst_ref=dst, send_sem=sems.at[0, i], recv_sem=sems.at[1, i],
            device_id=peer, device_id_type=pl.DeviceIdType.MESH,
        )

    chunks = gbuf.shape[0] // 2
    width = gbuf.shape[2]
    loads = []
    for part in range(2):
        base = (1 - core if part == 0 else core) * cols
        for q in range(chunks):
            j = part * chunks + q
            where = pl.ds(pl.multiple_of(base + q * width, HD), width)
            pair = (
                pltpu.make_async_copy(grad.at[0, :, where], gbuf.at[j], in_sem.at[0, j]),
                pltpu.make_async_copy(mom.at[0, :, where], mbuf.at[j], in_sem.at[1, j]),
            )
            pair[0].start()
            pair[1].start()
            loads.append(pair)
    y_cols = pl.ds(pl.multiple_of(y * HD, HD), HD)
    self_copies = (
        pltpu.make_async_copy(pseudo.at[0, :, y_cols], pself, p_sem.at[0]),
        pltpu.make_async_copy(outer.at[:, y_cols], pout, p_sem.at[1]),
    )
    for c in self_copies:
        c.start()

    def nesterov(j):
        for c in loads[j]:
            c.wait()
        g = gbuf[j].astype(f32)
        return (g + inner_beta * (inner_beta * mbuf[j].astype(f32) + g)).astype(bf16)

    sends = []
    core_copies = []
    for q in range(chunks):
        here = pl.ds(q * width, width)
        oth[:, here] = nesterov(q)
        if q == 0:
            pl.semaphore_wait(barrier, len(everyone))
        c = remote(oth.at[:, here], both.at[pl.ds(rows, rows), here], core_sem, q, sibling)
        c.start()
        core_copies.append(c)
    y_copies = {}
    for i, d in enumerate(y_order):
        if d:
            there = pl.ds(pl.multiple_of(lax.rem(y + d, ny) * HD, HD), HD)
            c = remote(pseudo.at[0, :, there], yr.at[i], y_sem, i, at_y(d))
            c.start()
            y_copies[i] = c
    for q in range(chunks):
        both[:rows, pl.ds(q * width, width)] = nesterov(chunks + q)
    for c in core_copies:
        c.wait_recv()

    upper, cross = masks()

    def gram(xo, d):
        at = pl.multiple_of((xo * nz + lax.rem(z + d, nz)) * HD, HD)
        block = both[:, pl.ds(at, HD)]
        full = lax.dot_general(block, block, (((0,), (0,)), ((), ())), preferred_element_type=f32)
        return pack(full, upper, cross)

    x_copies = []
    for i, d in enumerate(z_order):
        body, tail = gram(1 - xl, d)
        xs[i, :HALF, :] = body
        xs[i, HALF:, :] = tail
        c = remote(xs.at[i], xr.at[i], x_sem, i, x_peer)
        c.start()
        x_copies.append(c)
    for i, d in enumerate(z_order):
        body, tail = gram(xl, d)
        own[i, :HALF, :] = body
        own[i, HALF:, :] = tail
    z_copies = {}
    for i, d in enumerate(z_order):
        x_copies[i].wait_recv()
        own[i] = own[i] + xr[i]
        if d:
            c = remote(own.at[i], zr.at[i], z_sem, i, at_z(d))
            c.start()
            z_copies[i] = c

    for c in self_copies:
        c.wait()
    summed = pself[...].astype(f32)
    for i, c in y_copies.items():
        c.wait_recv()
        summed = summed + yr[i].astype(f32)
    half_own[...] = summed.astype(bf16)
    h_copy = remote(half_own, half_in, h_sem, 0, h_peer)
    h_copy.start()

    last = z_order.index(0)
    for i, c in z_copies.items():
        c.wait_recv()
        own[last] = own[last] + zr[i]
    eye = iota(0, HD) == iota(1, HD)
    tri = spread(own.at[last], upper, cross)
    tri = jnp.where(eye, 0.5 * tri, tri)
    matrix = tri + tri.T
    square = 2.0 * jnp.sum(jnp.where(eye, tri, 0.0), keepdims=True)
    scale = 1.0 / (jnp.sqrt(square) + norm_eps)
    matrix = matrix * scale * scale
    ident = jnp.where(eye, quint_a, 0.0)
    product = None
    for sweep in range(ITERS):
        squared = exact_dot(matrix, matrix)
        poly = ident + quint_b * matrix + quint_c * squared
        product = poly if product is None else exact_dot(product, poly)
        if sweep < ITERS - 1:
            matrix = exact_dot(exact_dot(poly, matrix), poly)
    product = product * (scale * math.sqrt(rows * lax.axis_size("fsdp")))
    body, tail = pack(jnp.where(eye, 0.5 * product, product), upper, cross)
    mz[last, :HALF, :] = body
    mz[last, HALF:, :] = tail
    m_copies = {}
    for i, d in enumerate(z_order):
        if d:
            c = remote(mz.at[last], mz.at[i], mz_sem, i, at_z(d))
            c.start()
            m_copies[i] = c

    h_copy.wait_recv()
    total = half_own[...].astype(f32) + half_in[...].astype(f32)
    fresh[...] = (
        outer_beta * pout[...].astype(f32) + total / lax.axis_size("rep")
    ).astype(bf16)
    r_local = pltpu.make_async_copy(fresh, renewed.at[:, y_cols], p_sem.at[2])
    r_local.start()
    r_copies = []
    for i, d in enumerate(y_order):
        if d:
            c = remote(fresh, renewed.at[:, y_cols], r_sem, i, at_y(d))
            c.start()
            r_copies.append(c)

    outs = []

    def finish(ref, block, head):
        tri = spread(ref, upper, cross)
        full = tri + tri.T
        high = full.astype(bf16)
        low = (full - high.astype(f32)).astype(bf16)
        res = jnp.dot(
            jnp.concatenate([block, block], axis=1),
            jnp.concatenate([high, low], axis=0),
            preferred_element_type=f32,
        ).astype(bf16)
        j = len(outs)
        out[j] = res
        at = pl.multiple_of(head * HD, HD)
        c = pltpu.make_async_copy(out.at[j], update.at[0, :, pl.ds(at, HD)], out_sem.at[j])
        c.start()
        outs.append(c)

    def place(xo, d):
        return xo * nz + lax.rem(z + nz - d, nz)

    def my_block(k):
        return both[:rows, pl.ds(pl.multiple_of(k * HD, HD), HD)]

    def oth_block(k):
        return oth[:, pl.ds(pl.multiple_of(k * HD, HD), HD)]

    near = list(reversed(list(enumerate(z_order))))
    s_copies = {}
    fx_copies = {}

    def got_z(step):
        i, d = near[step]
        if d:
            m_copies[i].wait_recv()
        fx_copies[i] = remote(mz.at[i], mx.at[i], mx_sem, i, x_peer)
        fx_copies[i].start()
        s_copies[i] = remote(mz.at[i], ms.at[i], ms_sem, i, sibling)
        s_copies[i].start()
        k = place(xl, d)
        finish(mz.at[i], my_block(k), core * heads + k)

    def got_x(step):
        i, d = near[step]
        fx_copies[i].wait_recv()
        s_copies[nz + i] = remote(mx.at[i], ms.at[nz + i], ms_sem, nz + i, sibling)
        s_copies[nz + i].start()
        k = place(1 - xl, d)
        finish(mx.at[i], my_block(k), core * heads + k)

    def got_s(step, other):
        i, d = near[step]
        s_copies[other * nz + i].wait_recv()
        k = place(1 - xl if other else xl, d)
        finish(ms.at[other * nz + i], oth_block(k), (1 - core) * heads + k)

    for step in range(nz + 2):
        if step < nz:
            got_z(step)
        if 1 <= step <= nz:
            got_s(step - 1, 0)
            got_x(step - 1)
        if step >= 2:
            got_s(step - 2, 1)

    for c in core_copies + x_copies + list(y_copies.values()) + list(z_copies.values()) + [h_copy]:
        c.wait_send()
    for c in list(m_copies.values()) + list(fx_copies.values()) + list(s_copies.values()):
        c.wait_send()
    for c in r_copies:
        c.wait()
    r_local.wait()
    for c in outs:
        c.wait()


def shards(gradient, momentum, pseudo_gradient, outer_momentum):
    fsdp, rep = lax.axis_size("fsdp"), lax.axis_size("rep")
    nz, ny = fsdp // 4, rep // 2
    _, rows, features = gradient.shape
    cols = features // 2
    heads = cols // HD
    chunks = 4
    width = cols // chunks
    vmem = pltpu.VMEM
    dma = pltpu.SemaphoreType.DMA
    hbm = pl.BlockSpec(memory_space=pl.ANY)
    packs = vmem((nz, PACK, HD), f32)
    column = vmem((rows, HD), bf16)
    return pl.pallas_call(
        functools.partial(kernel, nz, ny),
        out_shape=(
            jax.ShapeDtypeStruct(gradient.shape, bf16),
            jax.ShapeDtypeStruct(outer_momentum.shape, bf16),
        ),
        in_specs=[hbm] * 4,
        out_specs=(hbm, hbm),
        scratch_shapes=[
            vmem((2 * chunks, rows, width), bf16),
            vmem((2 * chunks, rows, width), bf16),
            vmem((rows, cols), bf16),
            vmem((2 * rows, cols), bf16),
            packs, packs, packs, packs,
            vmem((8, HD), f32),
            packs, packs,
            vmem((2 * nz, PACK, HD), f32),
            vmem((2 * heads, rows, HD), bf16),
            vmem((ny, rows, HD), bf16),
            column, column, column, column, column,
            dma((2, 2 * chunks)),
            dma((2, chunks)),
            dma((2, nz)),
            dma((2, nz)),
            dma((2, nz)),
            dma((2, nz)),
            dma((2, 2 * nz)),
            dma((2 * heads,)),
            dma((2, ny)),
            dma((2, 1)),
            dma((2, ny)),
            dma((3,)),
        ],
        compiler_params=pltpu.CompilerParams(
            collective_id=0, has_side_effects=True, vmem_limit_bytes=48 * 1024 * 1024
        ),
    )(gradient, momentum, pseudo_gradient, outer_momentum)


def solution(mesh):
    return jax.shard_map(
        shards,
        mesh=mesh,
        in_specs=(
            P("rep", "fsdp", None),
            P("rep", "fsdp", None),
            P("rep", "fsdp", None),
            P("fsdp", None),
        ),
        out_specs=(P("rep", "fsdp", None), P("fsdp", None)),
        check_vma=False,
    )
```

time: 335 us -> 64.5 us (0.19)
  the two profiles are of different devices: /device:TPU:8 before, /device:TPU:1 now
where the time goes in v1:
time: 64.5 us; the launch traced here: 64.3 us
  Pallas kernels  57.3 us (89%)
  local copies, waits for them, and re-layouts  6.35 us (10%)
  between operations  0.65 us (1%)
    pallas_call x1, Pallas kernels, shards(): pl.pallas_call(functools.partial(kernel, nz, ny), out_shape=(jax.ShapeDty...  57.3 us
    unnamed x10, local copies, waits for them, and re-layouts  6.35 us

profile of v1, /device:TPU:1, one launch (start us, length us, event | category | flops | bytes accessed | tf_op | source)
XLA Modules:
  0.0 64.3 jit_solution(7520891066614670893)
XLA Ops:
  0.6 0.0 copy-start
  0.6 1.3 %copy-done = bf16[1,160,4096]{2,1,0:T(8,128)(2,1)S(1)} copy-done((bf16[1,160,4096]{2,1,0:T(8,128)(2,1)S(1)}, bf16[1,160,4096]{2,1,0:T(8,128)(2,1)}, u32[]{:S(2)}) %copy-start) | copy-done | bytes 1310744
  1.9 0.0 copy-start.1
  1.9 1.3 %copy-done.1 = bf16[1,160,4096]{2,1,0:T(8,128)(2,1)S(1)} copy-done((bf16[1,160,4096]{2,1,0:T(8,128)(2,1)S(1)}, bf16[1,160,4096]{2,1,0:T(8,128)(2,1)}, u32[]{:S(2)}) %copy-start.1) | copy-done | bytes 1310744
  3.3 0.0 copy-start.2
  3.3 1.0 %copy-done.2 = bf16[1,160,1024]{2,1,0:T(8,128)(2,1)S(1)} copy-done((bf16[1,160,1024]{2,1,0:T(8,128)(2,1)S(1)}, bf16[1,160,1024]{2,1,0:T(8,128)(2,1)}, u32[]{:S(2)}) %copy-start.2) | copy-done | bytes 327704
  4.2 0.0 copy-start.3
  4.2 1.0 %copy-done.3 = bf16[160,1024]{1,0:T(8,128)(2,1)S(1)} copy-done((bf16[160,1024]{1,0:T(8,128)(2,1)S(1)}, bf16[160,1024]{1,0:T(8,128)(2,1)}, u32[]{:S(2)}) %copy-start.3) | copy-done | bytes 327704
  5.2 57.3 %shard_map.59 = (bf16[1,160,4096]{2,1,0:T(8,128)(2,1)S(1)}, bf16[160,1024]{1,0:T(8,128)(2,1)S(1)}) custom-call(bf16[1,160,4096]{2,1,0:T(8,128)(2,1)S(1)} %copy-done, bf16[1,160,4096]{2,1,0:T(8,128)(2,1)S(1)} %copy-done.1, bf16[1,160,1024]{2,1,0:T(8,128)(2,1)S(1)} %copy-done.2, bf16[160,1024]{1,0:T(8,128)(2,1)S(1)} %copy-done.3), custom_call_target="tpu_custom_call" | custom-call | tf_op jit(solution)/shard_map/pallas_call | solution.py:317
  62.5 1.1 %copy.8 = bf16[1,160,4096]{2,1,0:T(8,128)(2,1)} copy(bf16[1,160,4096]{2,1,0:T(8,128)(2,1)S(1)} %get-tuple-element.4) | data formatting | bytes 2621440
  63.6 0.7 %copy.9 = bf16[160,1024]{1,0:T(8,128)(2,1)} copy(bf16[160,1024]{1,0:T(8,128)(2,1)S(1)} %get-tuple-element.5) | data formatting | bytes 655360
Async XLA Ops:
  0.6 1.3 %copy-start = (bf16[1,160,4096]{2,1,0:T(8,128)(2,1)S(1)}, bf16[1,160,4096]{2,1,0:T(8,128)(2,1)}, u32[]{:S(2)}) copy-start(bf16[1,160,4096]{2,1,0:T(8,128)(2,1)} %grad.1) | copy-start | bytes 3932164
  1.9 1.3 %copy-start.1 = (bf16[1,160,4096]{2,1,0:T(8,128)(2,1)S(1)}, bf16[1,160,4096]{2,1,0:T(8,128)(2,1)}, u32[]{:S(2)}) copy-start(bf16[1,160,4096]{2,1,0:T(8,128)(2,1)} %mom.1) | copy-start | bytes 3932164
  3.3 1.0 %copy-start.2 = (bf16[1,160,1024]{2,1,0:T(8,128)(2,1)S(1)}, bf16[1,160,1024]{2,1,0:T(8,128)(2,1)}, u32[]{:S(2)}) copy-start(bf16[1,160,1024]{2,1,0:T(8,128)(2,1)} %pseudo.1) | copy-start | bytes 983044
  4.2 1.0 %copy-start.3 = (bf16[160,1024]{1,0:T(8,128)(2,1)S(1)}, bf16[160,1024]{1,0:T(8,128)(2,1)}, u32[]{:S(2)}) copy-start(bf16[160,1024]{1,0:T(8,128)(2,1)} %outer.1) | copy-start | bytes 983044

commit v2 on v1

--- a/solution.py
+++ b/solution.py
@@ -12,6 +12,7 @@
 HALF = HD // 2
 PACK = HALF + 8
 ITERS = 5
+DEPTH = 4
 
 quint_a = 3.4445
 quint_b = -4.775
@@ -56,7 +57,7 @@
 
 def kernel(
     nz, ny, grad, mom, pseudo, outer, update, renewed,
-    gbuf, mbuf, oth, both, xs, xr, own, zr, mine, mz, mx, ms, out,
+    gbuf, mbuf, oth, both, xs, xr, own, zr, mz, mx, ms, out,
     yr, pself, pout, half_own, half_in, fresh,
     in_sem, core_sem, x_sem, z_sem, mz_sem, mx_sem, ms_sem, out_sem, y_sem, h_sem, r_sem, p_sem,
 ):
@@ -129,6 +130,8 @@
         c = remote(oth.at[:, here], both.at[pl.ds(rows, rows), here], core_sem, q, sibling)
         c.start()
         core_copies.append(c)
+    for q in range(chunks):
+        both[:rows, pl.ds(q * width, width)] = nesterov(chunks + q)
     y_copies = {}
     for i, d in enumerate(y_order):
         if d:
@@ -136,52 +139,67 @@
             c = remote(pseudo.at[0, :, there], yr.at[i], y_sem, i, at_y(d))
             c.start()
             y_copies[i] = c
-    for q in range(chunks):
-        both[:rows, pl.ds(q * width, width)] = nesterov(chunks + q)
     for c in core_copies:
         c.wait_recv()
 
     upper, cross = masks()
 
     def gram(xo, d):
-        at = pl.multiple_of((xo * nz + lax.rem(z + d, nz)) * HD, HD)
+        at = pl.multiple_of((xo * nz + lax.rem(z + d + nz, nz)) * HD, HD)
         block = both[:, pl.ds(at, HD)]
         full = lax.dot_general(block, block, (((0,), (0,)), ((), ())), preferred_element_type=f32)
         return pack(full, upper, cross)
 
-    x_copies = []
+    def replica_sum():
+        for c in self_copies:
+            c.wait()
+        summed = pself[...].astype(f32)
+        for i, c in y_copies.items():
+            c.wait_recv()
+            summed = summed + yr[i].astype(f32)
+        half_own[...] = summed.astype(bf16)
+        copy = remote(half_own, half_in, h_sem, 0, h_peer)
+        copy.start()
+        return copy
+
+    def renew():
+        h_copy.wait_recv()
+        total = half_own[...].astype(f32) + half_in[...].astype(f32)
+        fresh[...] = (
+            outer_beta * pout[...].astype(f32) + total / lax.axis_size("rep")
+        ).astype(bf16)
+        copies = [pltpu.make_async_copy(fresh, renewed.at[:, y_cols], p_sem.at[2])]
+        for i, d in enumerate(y_order):
+            if d:
+                copies.append(remote(fresh, renewed.at[:, y_cols], r_sem, i, at_y(d)))
+        for c in copies:
+            c.start()
+        return copies
+
+    x_copies = [remote(xs.at[i], xr.at[i], x_sem, i, x_peer) for i in range(nz)]
     for i, d in enumerate(z_order):
-        body, tail = gram(1 - xl, d)
-        xs[i, :HALF, :] = body
-        xs[i, HALF:, :] = tail
-        c = remote(xs.at[i], xr.at[i], x_sem, i, x_peer)
-        c.start()
-        x_copies.append(c)
+        xs[i, :HALF, :], xs[i, HALF:, :] = gram(1 - xl, d)
+        if i < DEPTH:
+            x_copies[i].start()
     for i, d in enumerate(z_order):
-        body, tail = gram(xl, d)
-        own[i, :HALF, :] = body
-        own[i, HALF:, :] = tail
-    z_copies = {}
-    for i, d in enumerate(z_order):
+        own[i, :HALF, :], own[i, HALF:, :] = gram(xl, d)
+    z_copies = []
+    for i, d in enumerate(z_order[:-1]):
         x_copies[i].wait_recv()
         own[i] = own[i] + xr[i]
-        if d:
-            c = remote(own.at[i], zr.at[i], z_sem, i, at_z(d))
-            c.start()
-            z_copies[i] = c
-
-    for c in self_copies:
-        c.wait()
-    summed = pself[...].astype(f32)
-    for i, c in y_copies.items():
-        c.wait_recv()
-        summed = summed + yr[i].astype(f32)
-    half_own[...] = summed.astype(bf16)
-    h_copy = remote(half_own, half_in, h_sem, 0, h_peer)
-    h_copy.start()
-
-    last = z_order.index(0)
-    for i, c in z_copies.items():
+        z_copies.append(remote(own.at[i], zr.at[i], z_sem, i, at_z(d)))
+        z_copies[i].start()
+        if i + DEPTH < nz:
+            x_copies[i].wait_send()
+            x_copies[i + DEPTH].start()
+        if i == (nz - 1) // 2:
+            h_copy = replica_sum()
+
+    r_copies = renew()
+    last = nz - 1
+    x_copies[last].wait_recv()
+    own[last] = own[last] + xr[last]
+    for i, c in enumerate(z_copies):
         c.wait_recv()
         own[last] = own[last] + zr[i]
     eye = iota(0, HD) == iota(1, HD)
@@ -200,29 +218,7 @@
         if sweep < ITERS - 1:
             matrix = exact_dot(exact_dot(poly, matrix), poly)
     product = product * (scale * math.sqrt(rows * lax.axis_size("fsdp")))
-    body, tail = pack(jnp.where(eye, 0.5 * product, product), upper, cross)
-    mz[last, :HALF, :] = body
-    mz[last, HALF:, :] = tail
-    m_copies = {}
-    for i, d in enumerate(z_order):
-        if d:
-            c = remote(mz.at[last], mz.at[i], mz_sem, i, at_z(d))
-            c.start()
-            m_copies[i] = c
-
-    h_copy.wait_recv()
-    total = half_own[...].astype(f32) + half_in[...].astype(f32)
-    fresh[...] = (
-        outer_beta * pout[...].astype(f32) + total / lax.axis_size("rep")
-    ).astype(bf16)
-    r_local = pltpu.make_async_copy(fresh, renewed.at[:, y_cols], p_sem.at[2])
-    r_local.start()
-    r_copies = []
-    for i, d in enumerate(y_order):
-        if d:
-            c = remote(fresh, renewed.at[:, y_cols], r_sem, i, at_y(d))
-            c.start()
-            r_copies.append(c)
+    mz[0, :HALF, :], mz[0, HALF:, :] = pack(jnp.where(eye, 0.5 * product, product), upper, cross)
 
     outs = []
 
@@ -243,8 +239,8 @@
         c.start()
         outs.append(c)
 
-    def place(xo, d):
-        return xo * nz + lax.rem(z + nz - d, nz)
+    def place(xo, slot):
+        return xo * nz + lax.rem(z + nz - slot, nz)
 
     def my_block(k):
         return both[:rows, pl.ds(pl.multiple_of(k * HD, HD), HD)]
@@ -252,52 +248,61 @@
     def oth_block(k):
         return oth[:, pl.ds(pl.multiple_of(k * HD, HD), HD)]
 
-    near = list(reversed(list(enumerate(z_order))))
-    s_copies = {}
-    fx_copies = {}
-
-    def got_z(step):
-        i, d = near[step]
-        if d:
-            m_copies[i].wait_recv()
-        fx_copies[i] = remote(mz.at[i], mx.at[i], mx_sem, i, x_peer)
-        fx_copies[i].start()
-        s_copies[i] = remote(mz.at[i], ms.at[i], ms_sem, i, sibling)
-        s_copies[i].start()
-        k = place(xl, d)
-        finish(mz.at[i], my_block(k), core * heads + k)
-
-    def got_x(step):
-        i, d = near[step]
-        fx_copies[i].wait_recv()
-        s_copies[nz + i] = remote(mx.at[i], ms.at[nz + i], ms_sem, nz + i, sibling)
-        s_copies[nz + i].start()
-        k = place(1 - xl, d)
-        finish(mx.at[i], my_block(k), core * heads + k)
-
-    def got_s(step, other):
-        i, d = near[step]
-        s_copies[other * nz + i].wait_recv()
-        k = place(1 - xl if other else xl, d)
-        finish(ms.at[other * nz + i], oth_block(k), (1 - core) * heads + k)
-
-    for step in range(nz + 2):
-        if step < nz:
-            got_z(step)
-        if 1 <= step <= nz:
-            got_s(step - 1, 0)
-            got_x(step - 1)
-        if step >= 2:
-            got_s(step - 2, 1)
-
-    for c in core_copies + x_copies + list(y_copies.values()) + list(z_copies.values()) + [h_copy]:
-        c.wait_send()
-    for c in list(m_copies.values()) + list(fx_copies.values()) + list(s_copies.values()):
-        c.wait_send()
-    for c in r_copies:
-        c.wait()
-    r_local.wait()
-    for c in outs:
+    s_copies, fx_copies = {}, {}
+    near = list(reversed(z_order))
+    m_copies = {d: remote(mz.at[0], mz.at[d], mz_sem, d, at_z(d)) for d in near[1:]}
+
+    def got_z(slot):
+        if slot:
+            m_copies[slot].wait_recv()
+        fx_copies[slot] = remote(mz.at[slot], mx.at[slot], mx_sem, slot, x_peer)
+        fx_copies[slot].start()
+        s_copies[0, slot] = remote(mz.at[slot], ms.at[slot], ms_sem, slot, sibling)
+        s_copies[0, slot].start()
+        if slot == 0:
+            for c in m_copies.values():
+                c.start()
+            for c in core_copies + x_copies[max(nz - DEPTH, 0) :] + list(y_copies.values()):
+                c.wait_send()
+            for c in z_copies + [h_copy]:
+                c.wait_send()
+
+    def got_x(slot):
+        fx_copies[slot].wait_recv()
+        s_copies[1, slot] = remote(mx.at[slot], ms.at[nz + slot], ms_sem, nz + slot, sibling)
+        s_copies[1, slot].start()
+
+    def got_s(other, slot):
+        s_copies[other, slot].wait_recv()
+
+    groups = [[0]] + [near[k : k + 2] for k in range(1, nz, 2)]
+    for step in range(len(groups) + 2):
+        fresh_z = groups[step] if step < len(groups) else []
+        fresh_x = groups[step - 1] if 1 <= step <= len(groups) else []
+        late_x = groups[step - 2] if step >= 2 else []
+        for slot in fresh_z:
+            got_z(slot)
+        for slot in fresh_z:
+            k = place(xl, slot)
+            finish(mz.at[slot], my_block(k), core * heads + k)
+        for slot in fresh_x:
+            got_x(slot)
+        for slot in fresh_x:
+            k = place(1 - xl, slot)
+            finish(mx.at[slot], my_block(k), core * heads + k)
+        for slot in fresh_x:
+            got_s(0, slot)
+            k = place(xl, slot)
+            finish(ms.at[slot], oth_block(k), (1 - core) * heads + k)
+        for slot in late_x:
+            got_s(1, slot)
+            k = place(1 - xl, slot)
+            finish(ms.at[nz + slot], oth_block(k), (1 - core) * heads + k)
+
+    for group in (m_copies, fx_copies, s_copies):
+        for c in group.values():
+            c.wait_send()
+    for c in r_copies + outs:
         c.wait()
 
 
@@ -327,9 +332,7 @@
             vmem((2 * chunks, rows, width), bf16),
             vmem((rows, cols), bf16),
             vmem((2 * rows, cols), bf16),
-            packs, packs, packs, packs,
-            vmem((8, HD), f32),
-            packs, packs,
+            packs, packs, packs, packs, packs, packs,
             vmem((2 * nz, PACK, HD), f32),
             vmem((2 * heads, rows, HD), bf16),
             vmem((ny, rows, HD), bf16),
@@ -348,7 +351,7 @@
             dma((3,)),
         ],
         compiler_params=pltpu.CompilerParams(
-            collective_id=0, has_side_effects=True, vmem_limit_bytes=48 * 1024 * 1024
+            collective_id=0, has_side_effects=True, vmem_limit_bytes=60 * 1024 * 1024
         ),
     )(gradient, momentum, pseudo_gradient, outer_momentum)
 

time: 64.5 us -> 54.7 us (0.85)
  Pallas kernels: 57.3 us -> 50.6 us
  local copies, waits for them, and re-layouts: 6.35 us -> 3.26 us
    pallas_call x1, Pallas kernels: 57.3 us -> 50.6 us  [shards(): pl.pallas_call(functools.partial(kernel, nz, ny), out_shape=(jax.ShapeDty...]
    unnamed x10 -> x4, local copies, waits for them, and re-layouts: 6.35 us -> 3.26 us
where the time goes in v2:
time: 54.7 us; the launch traced here: 54.5 us
  Pallas kernels  50.6 us (93%)
  local copies, waits for them, and re-layouts  3.26 us (6%)
  between operations  0.65 us (1%)
    pallas_call x1, Pallas kernels, shards(): pl.pallas_call(functools.partial(kernel, nz, ny), out_shape=(jax.ShapeDty...  50.6 us
    unnamed x4, local copies, waits for them, and re-layouts  3.26 us

profile of v2, /device:TPU:1, one launch (start us, length us, event | category | flops | bytes accessed | tf_op | source)
XLA Modules:
  0.0 54.5 jit_solution(6662767620979328050)
XLA Ops:
  0.6 50.6 %shard_map.59 = (bf16[1,160,4096]{2,1,0:T(8,128)(2,1)}, bf16[160,1024]{1,0:T(8,128)(2,1)}) custom-call(bf16[1,160,4096]{2,1,0:T(8,128)(2,1)} %grad.1, bf16[1,160,4096]{2,1,0:T(8,128)(2,1)} %mom.1, bf16[1,160,1024]{2,1,0:T(8,128)(2,1)} %pseudo.1, bf16[160,1024]{1,0:T(8,128)(2,1)} %outer.1), custom_call_target="tpu_custom_call" | custom-call | tf_op jit(solution)/shard_map/pallas_call | solution.py:322
  51.2 0.0 copy-start
  51.2 2.5 %copy.8 = bf16[1,160,4096]{2,1,0:T(8,128)(2,1)} copy(bf16[1,160,4096]{2,1,0:T(8,128)(2,1)} %get-tuple-element.4) | data formatting | bytes 2621440
  53.8 0.0 copy-done
  53.8 0.7 %copy.9 = bf16[160,1024]{1,0:T(8,128)(2,1)} copy(bf16[160,1024]{1,0:T(8,128)(2,1)S(1)} %copy-done) | data formatting | bytes 655360
Async XLA Ops:
  51.2 2.5 %copy-start = (bf16[160,1024]{1,0:T(8,128)(2,1)S(1)}, bf16[160,1024]{1,0:T(8,128)(2,1)}, u32[]{:S(2)}) copy-start(bf16[160,1024]{1,0:T(8,128)(2,1)} %get-tuple-element.5) | copy-start | bytes 983044

commit v3 on v2

--- a/solution.py
+++ b/solution.py
@@ -57,9 +57,9 @@
 
 def kernel(
     nz, ny, grad, mom, pseudo, outer, update, renewed,
-    gbuf, mbuf, oth, both, xs, xr, own, zr, mz, mx, ms, out,
+    gbuf, mbuf, oth, both, xs, xr, own, zr, mz, mx, out,
     yr, pself, pout, half_own, half_in, fresh,
-    in_sem, core_sem, x_sem, z_sem, mz_sem, mx_sem, ms_sem, out_sem, y_sem, h_sem, r_sem, p_sem,
+    in_sem, core_sem, x_sem, z_sem, mz_sem, mx_sem, os_sem, out_sem, y_sem, h_sem, r_sem, p_sem,
 ):
     rep, fsdp = lax.axis_index("rep"), lax.axis_index("fsdp")
     core, xl, z = fsdp % 2, (fsdp // 2) % 2, fsdp // 4
@@ -80,10 +80,6 @@
     z_peers = [at_z(d) for d in range(1, nz)]
     y_peers = [at_y(d) for d in range(1, ny)]
     everyone = [sibling, x_peer, h_peer] + z_peers + y_peers
-
-    barrier = pltpu.get_barrier_semaphore()
-    for peer in everyone:
-        pl.semaphore_signal(barrier, inc=1, device_id=peer, device_id_type=pl.DeviceIdType.MESH)
 
     def remote(src, dst, sems, i, peer):
         return pltpu.make_async_remote_copy(
@@ -103,16 +99,18 @@
                 pltpu.make_async_copy(grad.at[0, :, where], gbuf.at[j], in_sem.at[0, j]),
                 pltpu.make_async_copy(mom.at[0, :, where], mbuf.at[j], in_sem.at[1, j]),
             )
-            pair[0].start()
-            pair[1].start()
+            if part == 0:
+                pair[0].start()
+                pair[1].start()
             loads.append(pair)
+    barrier = pltpu.get_barrier_semaphore()
+    for peer in everyone:
+        pl.semaphore_signal(barrier, inc=1, device_id=peer, device_id_type=pl.DeviceIdType.MESH)
     y_cols = pl.ds(pl.multiple_of(y * HD, HD), HD)
     self_copies = (
         pltpu.make_async_copy(pseudo.at[0, :, y_cols], pself, p_sem.at[0]),
         pltpu.make_async_copy(outer.at[:, y_cols], pout, p_sem.at[1]),
     )
-    for c in self_copies:
-        c.start()
 
     def nesterov(j):
         for c in loads[j]:
@@ -120,12 +118,13 @@
         g = gbuf[j].astype(f32)
         return (g + inner_beta * (inner_beta * mbuf[j].astype(f32) + g)).astype(bf16)
 
-    sends = []
     core_copies = []
     for q in range(chunks):
         here = pl.ds(q * width, width)
         oth[:, here] = nesterov(q)
         if q == 0:
+            for c in [c for pair in loads[chunks:] for c in pair] + list(self_copies):
+                c.start()
             pl.semaphore_wait(barrier, len(everyone))
         c = remote(oth.at[:, here], both.at[pl.ds(rows, rows), here], core_sem, q, sibling)
         c.start()
@@ -222,33 +221,31 @@
 
     outs = []
 
-    def finish(ref, block, head):
+    def finish(ref, k):
         tri = spread(ref, upper, cross)
         full = tri + tri.T
         high = full.astype(bf16)
         low = (full - high.astype(f32)).astype(bf16)
-        res = jnp.dot(
+        block = both[:, pl.ds(pl.multiple_of(k * HD, HD), HD)]
+        j = len(outs)
+        out[j] = jnp.dot(
             jnp.concatenate([block, block], axis=1),
             jnp.concatenate([high, low], axis=0),
             preferred_element_type=f32,
         ).astype(bf16)
-        j = len(outs)
-        out[j] = res
-        at = pl.multiple_of(head * HD, HD)
-        c = pltpu.make_async_copy(out.at[j], update.at[0, :, pl.ds(at, HD)], out_sem.at[j])
-        c.start()
-        outs.append(c)
+        at = update.at[0, :, pl.ds(pl.multiple_of((core * heads + k) * HD, HD), HD)]
+        pair = (
+            remote(out.at[j, pl.ds(rows, rows)], at, os_sem, j, sibling),
+            pltpu.make_async_copy(out.at[j, pl.ds(0, rows)], at, out_sem.at[j]),
+        )
+        for c in pair:
+            c.start()
+        outs.append(pair)
 
     def place(xo, slot):
         return xo * nz + lax.rem(z + nz - slot, nz)
 
-    def my_block(k):
-        return both[:rows, pl.ds(pl.multiple_of(k * HD, HD), HD)]
-
-    def oth_block(k):
-        return oth[:, pl.ds(pl.multiple_of(k * HD, HD), HD)]
-
-    s_copies, fx_copies = {}, {}
+    fx_copies = {}
     near = list(reversed(z_order))
     m_copies = {d: remote(mz.at[0], mz.at[d], mz_sem, d, at_z(d)) for d in near[1:]}
 
@@ -257,8 +254,6 @@
             m_copies[slot].wait_recv()
         fx_copies[slot] = remote(mz.at[slot], mx.at[slot], mx_sem, slot, x_peer)
         fx_copies[slot].start()
-        s_copies[0, slot] = remote(mz.at[slot], ms.at[slot], ms_sem, slot, sibling)
-        s_copies[0, slot].start()
         if slot == 0:
             for c in m_copies.values():
                 c.start()
@@ -267,43 +262,27 @@
             for c in z_copies + [h_copy]:
                 c.wait_send()
 
-    def got_x(slot):
-        fx_copies[slot].wait_recv()
-        s_copies[1, slot] = remote(mx.at[slot], ms.at[nz + slot], ms_sem, nz + slot, sibling)
-        s_copies[1, slot].start()
-
-    def got_s(other, slot):
-        s_copies[other, slot].wait_recv()
-
     groups = [[0]] + [near[k : k + 2] for k in range(1, nz, 2)]
-    for step in range(len(groups) + 2):
+    for step in range(len(groups) + 1):
         fresh_z = groups[step] if step < len(groups) else []
-        fresh_x = groups[step - 1] if 1 <= step <= len(groups) else []
-        late_x = groups[step - 2] if step >= 2 else []
+        fresh_x = groups[step - 1] if step else []
         for slot in fresh_z:
             got_z(slot)
         for slot in fresh_z:
-            k = place(xl, slot)
-            finish(mz.at[slot], my_block(k), core * heads + k)
+            finish(mz.at[slot], place(xl, slot))
         for slot in fresh_x:
-            got_x(slot)
+            fx_copies[slot].wait_recv()
         for slot in fresh_x:
-            k = place(1 - xl, slot)
-            finish(mx.at[slot], my_block(k), core * heads + k)
-        for slot in fresh_x:
-            got_s(0, slot)
-            k = place(xl, slot)
-            finish(ms.at[slot], oth_block(k), (1 - core) * heads + k)
-        for slot in late_x:
-            got_s(1, slot)
-            k = place(1 - xl, slot)
-            finish(ms.at[nz + slot], oth_block(k), (1 - core) * heads + k)
-
-    for group in (m_copies, fx_copies, s_copies):
+            finish(mx.at[slot], place(1 - xl, slot))
+
+    for group in (m_copies, fx_copies):
         for c in group.values():
             c.wait_send()
-    for c in r_copies + outs:
+    for c in r_copies:
         c.wait()
+    for pair in outs:
+        for c in pair:
+            c.wait()
 
 
 def shards(gradient, momentum, pseudo_gradient, outer_momentum):
@@ -316,7 +295,7 @@
     width = cols // chunks
     vmem = pltpu.VMEM
     dma = pltpu.SemaphoreType.DMA
-    hbm = pl.BlockSpec(memory_space=pl.ANY)
+    anywhere = pl.BlockSpec(memory_space=pl.ANY)
     packs = vmem((nz, PACK, HD), f32)
     column = vmem((rows, HD), bf16)
     return pl.pallas_call(
@@ -325,16 +304,15 @@
             jax.ShapeDtypeStruct(gradient.shape, bf16),
             jax.ShapeDtypeStruct(outer_momentum.shape, bf16),
         ),
-        in_specs=[hbm] * 4,
-        out_specs=(hbm, hbm),
+        in_specs=[pl.BlockSpec(memory_space=pltpu.HBM)] * 4,
+        out_specs=(anywhere, anywhere),
         scratch_shapes=[
             vmem((2 * chunks, rows, width), bf16),
             vmem((2 * chunks, rows, width), bf16),
             vmem((rows, cols), bf16),
             vmem((2 * rows, cols), bf16),
             packs, packs, packs, packs, packs, packs,
-            vmem((2 * nz, PACK, HD), f32),
-            vmem((2 * heads, rows, HD), bf16),
+            vmem((heads, 2 * rows, HD), bf16),
             vmem((ny, rows, HD), bf16),
             column, column, column, column, column,
             dma((2, 2 * chunks)),
@@ -343,8 +321,8 @@
             dma((2, nz)),
             dma((2, nz)),
             dma((2, nz)),
-            dma((2, 2 * nz)),
-            dma((2 * heads,)),
+            dma((2, heads)),
+            dma((heads,)),
             dma((2, ny)),
             dma((2, 1)),
             dma((2, ny)),

time: 54.7 us -> 53.4 us (0.976)
  Pallas kernels: 50.6 us -> 49.3 us
    pallas_call x1, Pallas kernels: 50.6 us -> 49.3 us  [shards(): pl.pallas_call(functools.partial(kernel, nz, ny), out_shape=(jax.ShapeDty...]
where the time goes in v3:
time: 53.4 us; the launch traced here: 53.2 us
  Pallas kernels  49.3 us (92%)
  local copies, waits for them, and re-layouts  3.26 us (6%)
  between operations  0.65 us (1%)
    pallas_call x1, Pallas kernels, shards(): pl.pallas_call(functools.partial(kernel, nz, ny), out_shape=(jax.ShapeDty...  49.3 us
    unnamed x4, local copies, waits for them, and re-layouts  3.26 us

profile of v3, /device:TPU:1, one launch (start us, length us, event | category | flops | bytes accessed | tf_op | source)
XLA Modules:
  0.0 53.2 jit_solution(11277644966426114459)
XLA Ops:
  0.6 49.3 %shard_map.59 = (bf16[1,160,4096]{2,1,0:T(8,128)(2,1)}, bf16[160,1024]{1,0:T(8,128)(2,1)}) custom-call(bf16[1,160,4096]{2,1,0:T(8,128)(2,1)} %grad.1, bf16[1,160,4096]{2,1,0:T(8,128)(2,1)} %mom.1, bf16[1,160,1024]{2,1,0:T(8,128)(2,1)} %pseudo.1, bf16[160,1024]{1,0:T(8,128)(2,1)} %outer.1), custom_call_target="tpu_custom_call" | custom-call | tf_op jit(solution)/shard_map/pallas_call | solution.py:301
  50.0 0.0 copy-start
  50.0 2.5 %copy.8 = bf16[1,160,4096]{2,1,0:T(8,128)(2,1)} copy(bf16[1,160,4096]{2,1,0:T(8,128)(2,1)} %get-tuple-element.4) | data formatting | bytes 2621440
  52.5 0.0 copy-done
  52.5 0.7 %copy.9 = bf16[160,1024]{1,0:T(8,128)(2,1)} copy(bf16[160,1024]{1,0:T(8,128)(2,1)S(1)} %copy-done) | data formatting | bytes 655360
Async XLA Ops:
  50.0 2.5 %copy-start = (bf16[160,1024]{1,0:T(8,128)(2,1)S(1)}, bf16[160,1024]{1,0:T(8,128)(2,1)}, u32[]{:S(2)}) copy-start(bf16[160,1024]{1,0:T(8,128)(2,1)} %get-tuple-element.5) | copy-start | bytes 983044

commit v4 on v3

--- a/solution.py
+++ b/solution.py
@@ -12,7 +12,6 @@
 HALF = HD // 2
 PACK = HALF + 8
 ITERS = 5
-DEPTH = 4
 
 quint_a = 3.4445
 quint_b = -4.775
@@ -175,32 +174,31 @@
             c.start()
         return copies
 
-    x_copies = [remote(xs.at[i], xr.at[i], x_sem, i, x_peer) for i in range(nz)]
-    for i, d in enumerate(z_order):
-        xs[i, :HALF, :], xs[i, HALF:, :] = gram(1 - xl, d)
-        if i < DEPTH:
-            x_copies[i].start()
-    for i, d in enumerate(z_order):
-        own[i, :HALF, :], own[i, HALF:, :] = gram(xl, d)
-    z_copies = []
-    for i, d in enumerate(z_order[:-1]):
-        x_copies[i].wait_recv()
-        own[i] = own[i] + xr[i]
-        z_copies.append(remote(own.at[i], zr.at[i], z_sem, i, at_z(d)))
-        z_copies[i].start()
-        if i + DEPTH < nz:
-            x_copies[i].wait_send()
-            x_copies[i + DEPTH].start()
-        if i == (nz - 1) // 2:
-            h_copy = replica_sum()
-
-    r_copies = renew()
     last = nz - 1
-    x_copies[last].wait_recv()
+    z_copies = {}
+    for half, xo, mine, theirs in ((0, 1 - xl, xs, xr), (1, xl, own, zr)):
+        for i, d in enumerate(z_order):
+            mine[i, :HALF, :], mine[i, HALF:, :] = gram(xo, d)
+            if d:
+                slot = half * nz + i
+                z_copies[half, i] = remote(mine.at[i], theirs.at[i], z_sem, slot, at_z(d))
+                z_copies[half, i].start()
+
+    def z_sum(half, mine, theirs):
+        total = mine[last]
+        for i in range(last):
+            z_copies[half, i].wait_recv()
+            total = total + theirs[i]
+        mine[last] = total
+
+    z_sum(0, xs, xr)
+    x_copy = remote(xs.at[last], xr.at[last], x_sem, 0, x_peer)
+    x_copy.start()
+    h_copy = replica_sum()
+    z_sum(1, own, zr)
+    x_copy.wait_recv()
     own[last] = own[last] + xr[last]
-    for i, c in enumerate(z_copies):
-        c.wait_recv()
-        own[last] = own[last] + zr[i]
+
     eye = iota(0, HD) == iota(1, HD)
     tri = spread(own.at[last], upper, cross)
     tri = jnp.where(eye, 0.5 * tri, tri)
@@ -245,39 +243,33 @@
     def place(xo, slot):
         return xo * nz + lax.rem(z + nz - slot, nz)
 
-    fx_copies = {}
+    fx_copy = remote(mz.at[0], mx.at[0], mx_sem, 0, x_peer)
+    fx_copy.start()
+    m_copies = {}
+    for half, blocks, sems in ((0, mz, mz_sem), (1, mx, mx_sem)):
+        if half:
+            r_copies = renew()
+            finish(mz.at[0], place(xl, 0))
+            fx_copy.wait_recv()
+        for d in z_order[:-1]:
+            m_copies[half, d] = remote(blocks.at[0], blocks.at[d], sems, d, at_z(d))
+            m_copies[half, d].start()
+    finish(mx.at[0], place(1 - xl, 0))
+    for c in core_copies + list(y_copies.values()) + list(z_copies.values()):
+        c.wait_send()
+    for c in (x_copy, h_copy, fx_copy):
+        c.wait_send()
+
     near = list(reversed(z_order))
-    m_copies = {d: remote(mz.at[0], mz.at[d], mz_sem, d, at_z(d)) for d in near[1:]}
-
-    def got_z(slot):
-        if slot:
-            m_copies[slot].wait_recv()
-        fx_copies[slot] = remote(mz.at[slot], mx.at[slot], mx_sem, slot, x_peer)
-        fx_copies[slot].start()
-        if slot == 0:
-            for c in m_copies.values():
-                c.start()
-            for c in core_copies + x_copies[max(nz - DEPTH, 0) :] + list(y_copies.values()):
-                c.wait_send()
-            for c in z_copies + [h_copy]:
-                c.wait_send()
-
-    groups = [[0]] + [near[k : k + 2] for k in range(1, nz, 2)]
-    for step in range(len(groups) + 1):
-        fresh_z = groups[step] if step < len(groups) else []
-        fresh_x = groups[step - 1] if step else []
-        for slot in fresh_z:
-            got_z(slot)
-        for slot in fresh_z:
-            finish(mz.at[slot], place(xl, slot))
-        for slot in fresh_x:
-            fx_copies[slot].wait_recv()
-        for slot in fresh_x:
-            finish(mx.at[slot], place(1 - xl, slot))
-
-    for group in (m_copies, fx_copies):
-        for c in group.values():
-            c.wait_send()
+    for half, blocks, xo in ((0, mz, xl), (1, mx, 1 - xl)):
+        for k in range(1, nz, 2):
+            for slot in near[k : k + 2]:
+                m_copies[half, slot].wait_recv()
+            for slot in near[k : k + 2]:
+                finish(blocks.at[slot], place(xo, slot))
+
+    for c in m_copies.values():
+        c.wait_send()
     for c in r_copies:
         c.wait()
     for pair in outs:
@@ -317,8 +309,8 @@
             column, column, column, column, column,
             dma((2, 2 * chunks)),
             dma((2, chunks)),
-            dma((2, nz)),
-            dma((2, nz)),
+            dma((2, 1)),
+            dma((2, 2 * nz)),
             dma((2, nz)),
             dma((2, nz)),
             dma((2, heads)),

time: 53.4 us -> 58.8 us (1.10)
  Pallas kernels: 49.3 us -> 54.7 us
    pallas_call x1, Pallas kernels: 49.3 us -> 54.7 us  [shards(): pl.pallas_call(functools.partial(kernel, nz, ny), out_shape=(jax.ShapeDty...]
where the time goes in v4:
time: 58.8 us; the launch traced here: 58.7 us
  Pallas kernels  54.7 us (93%)
  local copies, waits for them, and re-layouts  3.26 us (6%)
  between operations  0.65 us (1%)
    pallas_call x1, Pallas kernels, shards(): pl.pallas_call(functools.partial(kernel, nz, ny), out_shape=(jax.ShapeDty...  54.7 us
    unnamed x4, local copies, waits for them, and re-layouts  3.26 us

profile of v4, /device:TPU:1, one launch (start us, length us, event | category | flops | bytes accessed | tf_op | source)
XLA Modules:
  0.0 58.7 jit_solution(8605324267370475035)
XLA Ops:
  0.6 54.7 %shard_map.59 = (bf16[1,160,4096]{2,1,0:T(8,128)(2,1)}, bf16[160,1024]{1,0:T(8,128)(2,1)}) custom-call(bf16[1,160,4096]{2,1,0:T(8,128)(2,1)} %grad.1, bf16[1,160,4096]{2,1,0:T(8,128)(2,1)} %mom.1, bf16[1,160,1024]{2,1,0:T(8,128)(2,1)} %pseudo.1, bf16[160,1024]{1,0:T(8,128)(2,1)} %outer.1), custom_call_target="tpu_custom_call" | custom-call | tf_op jit(solution)/shard_map/pallas_call | solution.py:293
  55.4 0.0 copy-start
  55.4 2.5 %copy.8 = bf16[1,160,4096]{2,1,0:T(8,128)(2,1)} copy(bf16[1,160,4096]{2,1,0:T(8,128)(2,1)} %get-tuple-element.4) | data formatting | bytes 2621440
  57.9 0.0 copy-done
  57.9 0.7 %copy.9 = bf16[160,1024]{1,0:T(8,128)(2,1)} copy(bf16[160,1024]{1,0:T(8,128)(2,1)S(1)} %copy-done) | data formatting | bytes 655360
Async XLA Ops:
  55.4 2.5 %copy-start = (bf16[160,1024]{1,0:T(8,128)(2,1)S(1)}, bf16[160,1024]{1,0:T(8,128)(2,1)}, u32[]{:S(2)}) copy-start(bf16[160,1024]{1,0:T(8,128)(2,1)} %get-tuple-element.5) | copy-start | bytes 983044

commit v5 on v3

--- a/solution.py
+++ b/solution.py
@@ -191,10 +191,9 @@
         if i + DEPTH < nz:
             x_copies[i].wait_send()
             x_copies[i + DEPTH].start()
-        if i == (nz - 1) // 2:
-            h_copy = replica_sum()
-
-    r_copies = renew()
+
+    h_copy = replica_sum()
+
     last = nz - 1
     x_copies[last].wait_recv()
     own[last] = own[last] + xr[last]
@@ -245,7 +244,7 @@
     def place(xo, slot):
         return xo * nz + lax.rem(z + nz - slot, nz)
 
-    fx_copies = {}
+    fx_copies, r_copies = {}, []
     near = list(reversed(z_order))
     m_copies = {d: remote(mz.at[0], mz.at[d], mz_sem, d, at_z(d)) for d in near[1:]}
 
@@ -261,18 +260,18 @@
                 c.wait_send()
             for c in z_copies + [h_copy]:
                 c.wait_send()
+            r_copies.extend(renew())
 
     groups = [[0]] + [near[k : k + 2] for k in range(1, nz, 2)]
-    for step in range(len(groups) + 1):
-        fresh_z = groups[step] if step < len(groups) else []
-        fresh_x = groups[step - 1] if step else []
-        for slot in fresh_z:
+    for group in groups:
+        for slot in group:
             got_z(slot)
-        for slot in fresh_z:
+        for slot in group:
             finish(mz.at[slot], place(xl, slot))
-        for slot in fresh_x:
+    for group in groups:
+        for slot in group:
             fx_copies[slot].wait_recv()
-        for slot in fresh_x:
+        for slot in group:
             finish(mx.at[slot], place(1 - xl, slot))
 
     for group in (m_copies, fx_copies):

time: 53.4 us -> 50.6 us (0.948)
  Pallas kernels: 49.3 us -> 46.5 us
    pallas_call x1, Pallas kernels: 49.3 us -> 46.5 us  [shards(): pl.pallas_call(functools.partial(kernel, nz, ny), out_shape=(jax.ShapeDty...]
where the time goes in v5:
time: 50.6 us; the launch traced here: 50.4 us
  Pallas kernels  46.5 us (92%)
  local copies, waits for them, and re-layouts  3.26 us (6%)
  between operations  0.65 us (1%)
    pallas_call x1, Pallas kernels, shards(): pl.pallas_call(functools.partial(kernel, nz, ny), out_shape=(jax.ShapeDty...  46.5 us
    unnamed x4, local copies, waits for them, and re-layouts  3.26 us

profile of v5, /device:TPU:1, one launch (start us, length us, event | category | flops | bytes accessed | tf_op | source)
XLA Modules:
  0.0 50.4 jit_solution(416471459074681387)
XLA Ops:
  0.6 46.5 %shard_map.59 = (bf16[1,160,4096]{2,1,0:T(8,128)(2,1)}, bf16[160,1024]{1,0:T(8,128)(2,1)}) custom-call(bf16[1,160,4096]{2,1,0:T(8,128)(2,1)} %grad.1, bf16[1,160,4096]{2,1,0:T(8,128)(2,1)} %mom.1, bf16[1,160,1024]{2,1,0:T(8,128)(2,1)} %pseudo.1, bf16[160,1024]{1,0:T(8,128)(2,1)} %outer.1), custom_call_target="tpu_custom_call" | custom-call | tf_op jit(solution)/shard_map/pallas_call | solution.py:300
  47.1 0.0 copy-start
  47.1 2.5 %copy.8 = bf16[1,160,4096]{2,1,0:T(8,128)(2,1)} copy(bf16[1,160,4096]{2,1,0:T(8,128)(2,1)} %get-tuple-element.4) | data formatting | bytes 2621440
  49.7 0.0 copy-done
  49.7 0.7 %copy.9 = bf16[160,1024]{1,0:T(8,128)(2,1)} copy(bf16[160,1024]{1,0:T(8,128)(2,1)S(1)} %copy-done) | data formatting | bytes 655360
Async XLA Ops:
  47.1 2.5 %copy-start = (bf16[160,1024]{1,0:T(8,128)(2,1)S(1)}, bf16[160,1024]{1,0:T(8,128)(2,1)}, u32[]{:S(2)}) copy-start(bf16[160,1024]{1,0:T(8,128)(2,1)} %get-tuple-element.5) | copy-start | bytes 983044

commit v6 on v5

--- a/solution.py
+++ b/solution.py
@@ -246,7 +246,7 @@
 
     fx_copies, r_copies = {}, []
     near = list(reversed(z_order))
-    m_copies = {d: remote(mz.at[0], mz.at[d], mz_sem, d, at_z(d)) for d in near[1:]}
+    m_copies = {d: remote(mz.at[0], mz.at[d], mz_sem, d, at_z(d)) for d in z_order[:-1]}
 
     def got_z(slot):
         if slot:

time: 50.6 us -> 54.5 us (1.077)
  Pallas kernels: 46.5 us -> 50.4 us
    pallas_call x1, Pallas kernels: 46.5 us -> 50.4 us  [shards(): pl.pallas_call(functools.partial(kernel, nz, ny), out_shape=(jax.ShapeDty...]
where the time goes in v6:
time: 54.5 us; the launch traced here: 54.3 us
  Pallas kernels  50.4 us (92%)
  local copies, waits for them, and re-layouts  3.26 us (6%)
  between operations  0.65 us (1%)
    pallas_call x1, Pallas kernels, shards(): pl.pallas_call(functools.partial(kernel, nz, ny), out_shape=(jax.ShapeDty...  50.4 us
    unnamed x4, local copies, waits for them, and re-layouts  3.26 us

profile of v6, /device:TPU:1, one launch (start us, length us, event | category | flops | bytes accessed | tf_op | source)
XLA Modules:
  0.0 54.3 jit_solution(11540729347473187868)
XLA Ops:
  0.6 50.4 %shard_map.59 = (bf16[1,160,4096]{2,1,0:T(8,128)(2,1)}, bf16[160,1024]{1,0:T(8,128)(2,1)}) custom-call(bf16[1,160,4096]{2,1,0:T(8,128)(2,1)} %grad.1, bf16[1,160,4096]{2,1,0:T(8,128)(2,1)} %mom.1, bf16[1,160,1024]{2,1,0:T(8,128)(2,1)} %pseudo.1, bf16[160,1024]{1,0:T(8,128)(2,1)} %outer.1), custom_call_target="tpu_custom_call" | custom-call | tf_op jit(solution)/shard_map/pallas_call | solution.py:300
  51.1 0.0 copy-start
  51.1 2.5 %copy.8 = bf16[1,160,4096]{2,1,0:T(8,128)(2,1)} copy(bf16[1,160,4096]{2,1,0:T(8,128)(2,1)} %get-tuple-element.4) | data formatting | bytes 2621440
  53.6 0.0 copy-done
  53.6 0.7 %copy.9 = bf16[160,1024]{1,0:T(8,128)(2,1)} copy(bf16[160,1024]{1,0:T(8,128)(2,1)S(1)} %copy-done) | data formatting | bytes 655360
Async XLA Ops:
  51.1 2.5 %copy-start = (bf16[160,1024]{1,0:T(8,128)(2,1)S(1)}, bf16[160,1024]{1,0:T(8,128)(2,1)}, u32[]{:S(2)}) copy-start(bf16[160,1024]{1,0:T(8,128)(2,1)} %get-tuple-element.5) | copy-start | bytes 983044

commit v7 on v5

--- a/solution.py
+++ b/solution.py
@@ -12,7 +12,7 @@
 HALF = HD // 2
 PACK = HALF + 8
 ITERS = 5
-DEPTH = 4
+DEPTH = 8
 
 quint_a = 3.4445
 quint_b = -4.775

time: 50.6 us -> 50.7 us (level)
  no operation moved by 1% of the time
where the time goes in v7:
time: 50.7 us; the launch traced here: 50.6 us
  Pallas kernels  46.7 us (92%)
  local copies, waits for them, and re-layouts  3.26 us (6%)
  between operations  0.65 us (1%)
    pallas_call x1, Pallas kernels, shards(): pl.pallas_call(functools.partial(kernel, nz, ny), out_shape=(jax.ShapeDty...  46.7 us
    unnamed x4, local copies, waits for them, and re-layouts  3.26 us

profile of v7, /device:TPU:1, one launch (start us, length us, event | category | flops | bytes accessed | tf_op | source)
XLA Modules:
  0.0 50.6 jit_solution(786739569420409916)
XLA Ops:
  0.6 46.7 %shard_map.59 = (bf16[1,160,4096]{2,1,0:T(8,128)(2,1)}, bf16[160,1024]{1,0:T(8,128)(2,1)}) custom-call(bf16[1,160,4096]{2,1,0:T(8,128)(2,1)} %grad.1, bf16[1,160,4096]{2,1,0:T(8,128)(2,1)} %mom.1, bf16[1,160,1024]{2,1,0:T(8,128)(2,1)} %pseudo.1, bf16[160,1024]{1,0:T(8,128)(2,1)} %outer.1), custom_call_target="tpu_custom_call" | custom-call | tf_op jit(solution)/shard_map/pallas_call | solution.py:300
  47.3 0.0 copy-start
  47.3 2.5 %copy.8 = bf16[1,160,4096]{2,1,0:T(8,128)(2,1)} copy(bf16[1,160,4096]{2,1,0:T(8,128)(2,1)} %get-tuple-element.4) | data formatting | bytes 2621440
  49.8 0.0 copy-done
  49.9 0.7 %copy.9 = bf16[160,1024]{1,0:T(8,128)(2,1)} copy(bf16[160,1024]{1,0:T(8,128)(2,1)S(1)} %copy-done) | data formatting | bytes 655360
Async XLA Ops:
  47.3 2.5 %copy-start = (bf16[160,1024]{1,0:T(8,128)(2,1)S(1)}, bf16[160,1024]{1,0:T(8,128)(2,1)}, u32[]{:S(2)}) copy-start(bf16[160,1024]{1,0:T(8,128)(2,1)} %get-tuple-element.5) | copy-start | bytes 983044
